TPU v7x, 128 devices: a whole 4x4x4 slice. The times are simulated.
128 devices in a mesh: slab: 32 (over y_hi, x, z), dp: 4 (over y_lo, core).
Axes of the slice: x: 4, y: 4 (y_hi: 2, y_lo: 2; y = y_hi * 2 + y_lo), z: 4, core: 2. Of those that a mesh axis runs over, the one named last changes fastest.
Arguments:
- coarse_in: bfloat16 [4, 2, 64, 4, 8, 256], P('dp', None, 'slab'), may hold values from -6 to 6
- pre_up: bfloat16 [4, 2, 128, 8, 16, 128], P('dp', None, 'slab'), may hold values from -6 to 6
- pre_mid: bfloat16 [4, 2, 128, 8, 16, 128], P('dp', None, 'slab'), may hold values from -6 to 6
- grad_out: bfloat16 [4, 2, 128, 8, 16, 128], P('dp', None, 'slab'), may hold values from -6 to 6
- master: float32 [13824, 128], P(('slab', 'dp')), may hold values from -0.109375 to 0.109375
- moment: float32 [13824, 128], P(('slab', 'dp')), may hold values from -18 to 18
- second: float32 [13824, 128], P(('slab', 'dp')), may hold values from 1 to 30
Outputs:
- coarse_grad: bfloat16 [4, 2, 64, 4, 8, 256], P('dp', None, 'slab')
- new_master: float32 [13824, 128], P(('slab', 'dp'))
- new_moment: float32 [13824, 128], P(('slab', 'dp'))
- new_second: float32 [13824, 128], P(('slab', 'dp'))
All inputs are finite; a program needn't handle non-finite values.
Results may differ from a plain program's by a relative error of at most 0.0075.
Values may be sent and summed in bfloat16 or wider, within the bound.
A program may use at most 128 MiB of HBM per device.

v0:
```python
import jax
import jax.numpy as jnp
from jax import lax
from jax.sharding import PartitionSpec as P

beta_one = 0.9
beta_two = 0.999
adam_step = 10.0
learn_rate = 0.01
adam_eps = 1e-08


def padded_2(shard, sides, width):
    for axis, dim in sides:
        count, length = (lax.axis_size(axis), shard.shape[dim])
        up = [(i, (i + 1) % count) for i in range(count - 1)]
        down = [(j, i) for i, j in up]
        last = lax.slice_in_dim(shard, length - width, length, axis=dim)
        initial = lax.slice_in_dim(shard, 0, width, axis=dim)
        before = lax.ppermute(last, axis, up)
        after = lax.ppermute(initial, axis, down)
        shard = jnp.concatenate([before, shard, after], axis=dim)
    return shard


def from_behind(block, axis, distance):
    devices = range(lax.axis_size(axis))
    route = [(i - distance, i) for i in devices if i - distance in devices]
    return lax.ppermute(block, axis, route)


def correlate(padded, weight):
    samples_here, depth_ext, height, breadth, in_width = padded.shape
    inner_depth = depth_ext - 2
    lateral = jnp.pad(padded, ((0, 0), (0, 0), (1, 1), (1, 1), (0, 0)))
    running = None
    for depth_tap in range(3):
        for row_tap in range(3):
            columns = jnp.concatenate(
                [
                    lateral[
                        :,
                        depth_tap : depth_tap + inner_depth,
                        row_tap : row_tap + height,
                        col_tap : col_tap + breadth,
                        :,
                    ]
                    for col_tap in range(3)
                ],
                axis=-1,
            )
            row_start = (depth_tap * 3 + row_tap) * 3 * in_width
            product_term = jnp.dot(
                columns.reshape(-1, 3 * in_width),
                weight[row_start : row_start + 3 * in_width],
                preferred_element_type=jnp.float32,
            )
            running = product_term if running is None else running + product_term
    return running.reshape(samples_here, inner_depth, height, breadth, weight.shape[1])


def filter_grad(padded, grads):
    samples_here, depth_ext, height, breadth, in_width = padded.shape
    inner_depth = depth_ext - 2
    lateral = jnp.pad(padded, ((0, 0), (0, 0), (1, 1), (1, 1), (0, 0)))
    flat_grads = grads.reshape(-1, grads.shape[-1])
    blocks = []
    for depth_tap in range(3):
        for row_tap in range(3):
            columns = jnp.concatenate(
                [
                    lateral[
                        :,
                        depth_tap : depth_tap + inner_depth,
                        row_tap : row_tap + height,
                        col_tap : col_tap + breadth,
                        :,
                    ]
                    for col_tap in range(3)
                ],
                axis=-1,
            )
            blocks.append(
                lax.dot_general(
                    columns.reshape(-1, 3 * in_width),
                    flat_grads,
                    (((0,), (0,)), ((), ())),
                    preferred_element_type=jnp.float32,
                )
            )
    return jnp.concatenate(blocks, axis=0)


def flipped(weight, in_width):
    out_width = weight.shape[1]
    shaped = weight.reshape(3, 3, 3, in_width, out_width)[::-1, ::-1, ::-1]
    return shaped.transpose(0, 1, 2, 4, 3).reshape(27 * out_width, in_width)


def upconv_back(grad_pad, coarse, weight):
    lateral = jnp.pad(grad_pad, ((0, 0), (0, 0), (1, 0), (1, 0), (0, 0)))
    samples_here, coarse_depth, coarse_rows, coarse_cols, coarse_width = coarse.shape
    fine_width = weight.shape[1]
    slices = []
    for depth_tap in range(3):
        for row_tap in range(3):
            for col_tap in range(3):
                slices.append(
                    lateral[
                        :,
                        depth_tap : depth_tap + 2 * coarse_depth : 2,
                        row_tap : row_tap + 2 * coarse_rows : 2,
                        col_tap : col_tap + 2 * coarse_cols : 2,
                        :,
                    ]
                )
    gathered = jnp.concatenate(slices, axis=-1).reshape(-1, 27 * fine_width)
    turned = (
        weight.reshape(27, coarse_width, fine_width)
        .transpose(0, 2, 1)
        .reshape(27 * fine_width, coarse_width)
    )
    coarse_grad = jnp.dot(gathered, turned, preferred_element_type=jnp.float32).reshape(
        coarse.shape
    )
    filter_part = lax.dot_general(
        coarse.reshape(-1, coarse_width),
        gathered,
        (((0,), (0,)), ((), ())),
        preferred_element_type=jnp.float32,
    )
    filter_part = (
        filter_part.reshape(coarse_width, 27, fine_width)
        .transpose(1, 0, 2)
        .reshape(27 * coarse_width, fine_width)
    )
    return (coarse_grad, filter_part)


def body(coarse_in, pre_up, pre_mid, grad_out, master, moment, second):
    channels = pre_up.shape[-1]
    group_size = pre_up.shape[1]
    shards = lax.all_gather(master.astype(jnp.bfloat16), ("slab", "dp"), axis=0, tiled=True)
    w_one = shards[: 27 * channels]
    w_two = shards[27 * channels : 54 * channels]
    w_up = shards[54 * channels :]
    flip_one = flipped(w_one, channels)
    flip_two = flipped(w_two, channels)
    up_in = pre_up.reshape((-1,) + pre_up.shape[2:])
    mid_in = pre_mid.reshape((-1,) + pre_mid.shape[2:])
    out_in = grad_out.reshape((-1,) + grad_out.shape[2:])
    rim_block = padded_2(jnp.stack([jax.nn.relu(mid_in), out_in]), (("slab", 2),), 1)
    mid_act = rim_block[0]
    out_pad = rim_block[1]
    grad_two = filter_grad(mid_act, out_in)
    back_mid = correlate(out_pad, flip_two)
    mid_grad = jnp.where(mid_in > 0, back_mid, 0.0).astype(jnp.bfloat16)
    inner_rims = padded_2(jnp.stack([jax.nn.relu(up_in), mid_grad]), (("slab", 2),), 1)
    up_act = inner_rims[0]
    mid_grad_pad = inner_rims[1]
    grad_one = filter_grad(up_act, mid_grad)
    back_up = correlate(mid_grad_pad, flip_one)
    up_grad = jnp.where(up_in > 0, back_up, 0.0).astype(jnp.bfloat16)
    previous = from_behind(up_grad[:, -1:], "slab", 1)
    grad_pad = jnp.concatenate([previous, up_grad], axis=1)
    coarse_here = coarse_in.reshape((-1,) + coarse_in.shape[2:])
    coarse_grad, grad_up = upconv_back(grad_pad, coarse_here, w_up)
    coarse_grad = coarse_grad.astype(jnp.bfloat16).reshape(coarse_in.shape)
    partial_value = jnp.concatenate([grad_one, grad_two, grad_up], axis=0)
    totals = lax.psum(partial_value, ("slab", "dp"))
    own_rows = master.shape[0]
    summed = lax.dynamic_slice_in_dim(
        totals, lax.axis_index(("slab", "dp")) * own_rows, own_rows, 0
    )
    mean_grad = summed / float(group_size * lax.axis_size("dp"))
    new_moment = beta_one * moment + (1.0 - beta_one) * mean_grad
    new_second = beta_two * second + (1.0 - beta_two) * mean_grad * mean_grad
    corrected = new_moment / (1.0 - beta_one**adam_step)
    scaled = jnp.sqrt(new_second / (1.0 - beta_two**adam_step)) + adam_eps
    new_master = master - learn_rate * corrected / scaled
    return (coarse_grad, new_master, new_moment, new_second)


def solution(mesh):
    return jax.shard_map(
        body,
        mesh=mesh,
        in_specs=(
            P("dp", None, "slab", None, None, None),
            P("dp", None, "slab", None, None, None),
            P("dp", None, "slab", None, None, None),
            P("dp", None, "slab", None, None, None),
            P(("slab", "dp"), None),
            P(("slab", "dp"), None),
            P(("slab", "dp"), None),
        ),
        out_specs=(
            P("dp", None, "slab", None, None, None),
            P(("slab", "dp"), None),
            P(("slab", "dp"), None),
            P(("slab", "dp"), None),
        ),
        check_vma=False,
    )
```

profile of v0, /device:TPU:1, one launch (start us, length us, event | category | flops | bytes accessed | tf_op | source)
XLA Modules:
  0.0 458.4 jit_solution(18084580664319161008)
XLA Ops:
  7.2 1.5 convert_bitcast_fusion
  10.7 1.3 collective-permute-start.1
  12.0 5.0 %collective-permute-start = (bf16[2,2,1,8,16,128]{5,4,3,2,1,0:T(8,128)(2,1)S(1)}, bf16[2,2,1,8,16,128]{5,4,3,2,1,0:T(8,128)(2,1)S(1)}, u32[]{:S(2)}, u32[]{:S(2)}) collective-permute-start(bf16[2,2,1,8,16,128]{5,4,3,2,1,0:T(8,128)(2,1)S(1)} %get-tuple-element.15), channel_id=1, source_target_pairs={{0,4},{4,8},{8,12},{12,16},{16,20},{20,24},{24,28},{28,32},{32,36}... | collective-permute-start | bytes 393224 | tf_op jit(solution)/shard_map/ppermute | solution.py:20
  32.9 1.4 pad_maximum_fusion.3
  34.3 1.5 pad_maximum_fusion.6
  35.8 1.4 pad_maximum_fusion.22
  37.2 1.4 pad_maximum_fusion.25
  38.6 172.9 %all-gather.3.cloned.1.call-done = bf16[128,108,128]{2,1,0:T(8,128)(2,1)} async-done(((bf16[1,108,128]{2,1,0:T(8,128)(2,1)}), bf16[128,108,128]{2,1,0:T(8,128)(2,1)}) %all-gather.3.cloned.1.call-update) | async-done | bytes 3538960 | tf_op jit(solution)/shard_map/all_gather | solution.py:143
  211.5 1.6 fusion.90
  213.3 1.4 copy.17
  214.7 1.6 fusion.79
  222.0 1.3 collective-permute-start.3
  223.3 4.6 %collective-permute-start.2 = (bf16[2,2,1,8,16,128]{5,4,3,2,1,0:T(8,128)(2,1)}, bf16[2,2,1,8,16,128]{5,4,3,2,1,0:T(8,128)(2,1)}, u32[]{:S(2)}, u32[]{:S(2)}) collective-permute-start(bf16[2,2,1,8,16,128]{5,4,3,2,1,0:T(8,128)(2,1)} %get-tuple-element.13), channel_id=1, source_target_pairs={{0,4},{4,8},{8,12},{12,16},{16,20},{20,24},{24,28},{28,32},{32,36}... | collective-permute-start | bytes 393224 | tf_op jit(solution)/shard_map/ppermute | solution.py:20
  228.2 1.4 copy.18
  239.3 3.8 collective-permute-start.4
  251.7 2.9 copy-done.2
  269.2 2.4 fusion.91
  271.6 5.2 %copy.20 = f32[27,256,128]{2,1,0:T(8,128)} copy(f32[27,256,128]{1,2,0:T(8,128)} %bitcast.181) | data formatting | bytes 7077888 | tf_op jit(solution)/shard_map/transpose | solution.py:134
  276.8 4.1 constant_dynamic-update-slice_fusion.27
  280.9 1.5 slice-done
  282.4 1.4 reshape.171
  283.8 2.6 copy.19
  287.5 162.5 %all-reduce.7.cloned.1.call-done = f32[13824,128]{1,0:T(8,128)} async-done(((f32[13824,128]{1,0:T(8,128)}), f32[13824,128]{1,0:T(8,128)}) %all-reduce.7.cloned.1.call-update) | async-done | bytes 7077904 | tf_op jit(solution)/shard_map/psum | solution.py:170
  450.0 1.5 divide_subtract_fusion
  (198 shorter events, 56.9 us)
Async XLA Ops:
  7.2 262.0 %copy-start = (bf16[1,2,2,4,8,256]{5,4,3,2,1,0:T(8,128)(2,1)S(1)}, bf16[1,2,2,4,8,256]{5,4,3,2,1,0:T(8,128)(2,1)}, u32[]{:S(2)}) copy-start(bf16[1,2,2,4,8,256]{5,4,3,2,1,0:T(8,128)(2,1)} %param.7) | copy-start | bytes 196612
  7.2 12.0 %copy-start.1 = (bf16[1,2,4,8,16,128]{5,4,3,2,1,0:T(8,128)(2,1)S(1)}, bf16[1,2,4,8,16,128]{5,4,3,2,1,0:T(8,128)(2,1)}, u32[]{:S(2)}) copy-start(bf16[1,2,4,8,16,128]{5,4,3,2,1,0:T(8,128)(2,1)} %param.10) | copy-start | bytes 786436
  7.2 9.8 %copy-start.23 = (bf16[1,2,4,8,16,128]{5,4,3,2,1,0:T(8,128)(2,1)S(1)}, bf16[1,2,4,8,16,128]{5,4,3,2,1,0:T(8,128)(2,1)}, u32[]{:S(2)}) copy-start(bf16[1,2,4,8,16,128]{5,4,3,2,1,0:T(8,128)(2,1)} %param.8) | copy-start | bytes 786436
  7.2 204.3 %all-gather.3.cloned.1.call-start = ((), (), s32[]{:S(2)}) async-start(), calls=%async_computation.1 | async-start | bytes 3698688 | tf_op jit(solution)/shard_map/all_gather | solution.py:143
  8.8 441.2 %all-reduce.7.cloned.1.call-start = ((), (), s32[]{:S(2)}) async-start(), calls=%async_computation | async-start | bytes 14155776 | tf_op jit(solution)/shard_map/psum | solution.py:170
  10.7 7.6 %collective-permute-start.1 = (bf16[2,2,1,8,16,128]{5,4,3,2,1,0:T(8,128)(2,1)S(1)}, bf16[2,2,1,8,16,128]{5,4,3,2,1,0:T(8,128)(2,1)S(1)}, u32[]{:S(2)}, u32[]{:S(2)}) collective-permute-start(bf16[2,2,1,8,16,128]{5,4,3,2,1,0:T(8,128)(2,1)S(1)} %get-tuple-element.16), channel_id=1, source_target_pairs={{4,0},{8,4},{12,8},{16,12},{20,16},{24,20},{28,24},{32,28},{36,32}... | collective-permute-start | bytes 393224 | tf_op jit(solution)/shard_map/ppermute | solution.py:21
  12.0 7.1 %collective-permute-start = (bf16[2,2,1,8,16,128]{5,4,3,2,1,0:T(8,128)(2,1)S(1)}, bf16[2,2,1,8,16,128]{5,4,3,2,1,0:T(8,128)(2,1)S(1)}, u32[]{:S(2)}, u32[]{:S(2)}) collective-permute-start(bf16[2,2,1,8,16,128]{5,4,3,2,1,0:T(8,128)(2,1)S(1)} %get-tuple-element.15), channel_id=1, source_target_pairs={{0,4},{4,8},{8,12},{12,16},{16,20},{20,24},{24,28},{28,32},{32,36}... | collective-permute-start | bytes 393224 | tf_op jit(solution)/shard_map/ppermute | solution.py:20
  214.7 1.6 copy-start.15
  214.7 2.0 copy-start.18
  222.0 7.7 %collective-permute-start.3 = (bf16[2,2,1,8,16,128]{5,4,3,2,1,0:T(8,128)(2,1)}, bf16[2,2,1,8,16,128]{5,4,3,2,1,0:T(8,128)(2,1)}, u32[]{:S(2)}, u32[]{:S(2)}) collective-permute-start(bf16[2,2,1,8,16,128]{5,4,3,2,1,0:T(8,128)(2,1)} %get-tuple-element.14), channel_id=1, source_target_pairs={{4,0},{8,4},{12,8},{16,12},{20,16},{24,20},{28,24},{32,28},{36,32}... | collective-permute-start | bytes 393224 | tf_op jit(solution)/shard_map/ppermute | solution.py:21
  223.3 6.4 %collective-permute-start.2 = (bf16[2,2,1,8,16,128]{5,4,3,2,1,0:T(8,128)(2,1)}, bf16[2,2,1,8,16,128]{5,4,3,2,1,0:T(8,128)(2,1)}, u32[]{:S(2)}, u32[]{:S(2)}) collective-permute-start(bf16[2,2,1,8,16,128]{5,4,3,2,1,0:T(8,128)(2,1)} %get-tuple-element.13), channel_id=1, source_target_pairs={{0,4},{4,8},{8,12},{12,16},{16,20},{20,24},{24,28},{28,32},{32,36}... | collective-permute-start | bytes 393224 | tf_op jit(solution)/shard_map/ppermute | solution.py:20
  228.2 1.5 copy-start.22
  239.3 15.4 %collective-permute-start.4 = (bf16[2,1,8,16,128]{4,3,2,1,0:T(8,128)(2,1)S(1)}, bf16[2,1,8,16,128]{4,3,2,1,0:T(8,128)(2,1)S(1)}, u32[]{:S(2)}, u32[]{:S(2)}) collective-permute-start(bf16[2,1,8,16,128]{4,3,2,1,0:T(8,128)(2,1)S(1)} %slice.703), channel_id=1, source_target_pairs={{0,4},{4,8},{8,12},{12,16},{16,20},{20,24},{24,28},{28,32},{32,36}... | collective-permute-start | bytes 196616 | tf_op jit(solution)/shard_map/ppermute | solution.py:29
  246.6 1.6 copy-start.7
  247.0 1.6 copy-start.11
  248.1 1.3 copy-start.5
  248.6 1.3 copy-start.12
  249.0 1.3 copy-start.10
  249.5 1.3 copy-start.3
  251.7 3.0 copy-start.2
  280.9 1.5 slice-start
  286.4 163.6 %copy-start.25 = (f32[108,128]{1,0:T(8,128)S(1)}, f32[108,128]{1,0:T(8,128)}, u32[]{:S(2)}) copy-start(f32[108,128]{1,0:T(8,128)} %param.11) | copy-start | bytes 165892
  286.5 163.5 %copy-start.26 = (f32[108,128]{1,0:T(8,128)S(1)}, f32[108,128]{1,0:T(8,128)}, u32[]{:S(2)}) copy-start(f32[108,128]{1,0:T(8,128)} %param.12) | copy-start | bytes 165892
  286.5 163.5 %copy-start.27 = (f32[108,128]{1,0:T(8,128)S(1)}, f32[108,128]{1,0:T(8,128)}, u32[]{:S(2)}) copy-start(f32[108,128]{1,0:T(8,128)} %param.13) | copy-start | bytes 165892
  (12 other events, 13.8 us)
Sparse Core Ops, SparseCore 0:
  10.3 201.1 all-gather.2
  281.1 168.8 all-reduce.6
where the time goes:
time: 459 us; the launch traced here: 458 us
  waiting for transfers between devices  337 us (73%)
  local copies, waits for them, and re-layouts  46.5 us (10%)
  other arithmetic  24.8 us (5%)
  matrix products  18.9 us (4%)
  starting transfers between devices  16.1 us (4%)
  between operations  15.3 us (3%)
    all_gather x1, waiting for transfers between devices, body(): lax.all_gather(master.astype(jnp.bfloat16), ('slab', 'dp'), axis=0, tiled...  173 us
    psum x1, waiting for transfers between devices, body(): totals = lax.psum(partial_value, ('slab', 'dp'))  162 us
    slice x27, local copies, waits for them, and re-layouts, upconv_back(): lateral[:, depth_tap:depth_tap + 2 * coarse_depth:2, row_tap:row_tap + 2...  13.7 us
    ppermute x2, starting transfers between devices, padded_2(): before = lax.ppermute(last, axis, up)  9.65 us
  transfers between devices with their start and end apart: 7, of which 4 were waited for; matrix products, arithmetic and copies ran while one was open for 8% of the time, Pallas kernels for 0%

commit v1 on v0

--- a/solution.py
+++ b/solution.py
@@ -140,7 +140,15 @@
 def body(coarse_in, pre_up, pre_mid, grad_out, master, moment, second):
     channels = pre_up.shape[-1]
     group_size = pre_up.shape[1]
-    shards = lax.all_gather(master.astype(jnp.bfloat16), ("slab", "dp"), axis=0, tiled=True)
+    shards = jnp.concatenate(
+        lax.all_to_all(
+            jnp.stack([master.astype(jnp.bfloat16)] * lax.axis_size(("slab", "dp"))),
+            ("slab", "dp"),
+            0,
+            0,
+        ),
+        axis=0,
+    )
     w_one = shards[: 27 * channels]
     w_two = shards[27 * channels : 54 * channels]
     w_up = shards[54 * channels :]

time: 459 us -> 336 us (0.73)
  waiting for transfers between devices: 337 us -> 203 us
  starting transfers between devices: 16.1 us -> 27 us
    all_gather x1 -> x0, waiting for transfers between devices: 173 us -> none  [body(): lax.all_gather(master.astype(jnp.bfloat16), ('slab', 'dp'), axis=0, tiled...]
    ppermute x2, waiting for transfers between devices: 0.54 us -> 40.1 us  [padded_2(): after = lax.ppermute(initial, axis, down)]
    all_to_all x0 -> x1, starting transfers between devices: none -> 11.9 us  [body(): lax.all_to_all(jnp.stack([master.astype(jnp.bfloat16)] * lax.axis_size(('...]
  transfers between devices with their start and end apart: 7 -> 7, of which waited for: 4 -> 2; matrix products, arithmetic and copies ran while one was open for 8% -> 11% of each run, Pallas kernels for 0% -> 0%
where the time goes in v1:
time: 336 us; the launch traced here: 335 us
  waiting for transfers between devices  203 us (60%)
  local copies, waits for them, and re-layouts  48.9 us (15%)
  starting transfers between devices  27 us (8%)
  other arithmetic  22.2 us (7%)
  matrix products  18.9 us (6%)
  between operations  15.3 us (5%)
    psum x1, waiting for transfers between devices, body(): totals = lax.psum(partial_value, ('slab', 'dp'))  163 us
    ppermute x2, waiting for transfers between devices, padded_2(): after = lax.ppermute(initial, axis, down)  40.1 us
    slice x27, local copies, waits for them, and re-layouts, upconv_back(): lateral[:, depth_tap:depth_tap + 2 * coarse_depth:2, row_tap:row_tap + 2...  13.7 us
    all_to_all x1, starting transfers between devices, body(): lax.all_to_all(jnp.stack([master.astype(jnp.bfloat16)] * lax.axis_size(('...  11.9 us
    concatenate x16, other arithmetic, correlate(): jnp.concatenate([lateral[:, depth_tap:depth_tap + inner_depth, row_tap:ro...  8.79 us
    ppermute x2, starting transfers between devices, padded_2(): before = lax.ppermute(last, axis, up)  8.68 us
    concatenate x7, other arithmetic, filter_grad(): jnp.concatenate([lateral[:, depth_tap:depth_tap + inner_depth, row_tap:ro...  7.92 us
    dot_general x18, matrix products, correlate(): jnp.dot(columns.reshape(-1, 3 * in_width), weight[row_start:row_start + 3...  7.8 us
  transfers between devices with their start and end apart: 7, of which 2 were waited for; matrix products, arithmetic and copies ran while one was open for 11% of the time, Pallas kernels for 0%

profile of v1, /device:TPU:1, one launch (start us, length us, event | category | flops | bytes accessed | tf_op | source)
XLA Modules:
  0.0 335.4 jit_solution(6067333080668229953)
XLA Ops:
  8.0 2.3 stack.7
  10.3 11.9 %all-to-all-start = ((bf16[128,108,128]{2,1,0:T(8,128)(2,1)}), bf16[128,108,128]{2,1,0:T(8,128)(2,1)}, u32[]{:S(2)}, u32[]{:S(2)}) async-start(bf16[128,108,128]{2,1,0:T(8,128)(2,1)} %stack.7), calls=%async_computation | async-start | bytes 7340032 | tf_op jit(solution)/shard_map/all_to_all | solution.py:144
  22.3 1.3 collective-permute-start.1
  23.6 4.0 %collective-permute-start = (bf16[2,2,1,8,16,128]{5,4,3,2,1,0:T(8,128)(2,1)S(1)}, bf16[2,2,1,8,16,128]{5,4,3,2,1,0:T(8,128)(2,1)S(1)}, u32[]{:S(2)}, u32[]{:S(2)}) collective-permute-start(bf16[2,2,1,8,16,128]{5,4,3,2,1,0:T(8,128)(2,1)S(1)} %get-tuple-element.15), channel_id=1, source_target_pairs={{0,4},{4,8},{8,12},{12,16},{16,20},{20,24},{24,28},{28,32},{32,36}... | collective-permute-start | bytes 393224 | tf_op jit(solution)/shard_map/ppermute | solution.py:20
  28.5 40.1 %collective-permute-done.1 = bf16[2,2,1,8,16,128]{5,4,3,2,1,0:T(8,128)(2,1)S(1)} collective-permute-done((bf16[2,2,1,8,16,128]{5,4,3,2,1,0:T(8,128)(2,1)S(1)}, bf16[2,2,1,8,16,128]{5,4,3,2,1,0:T(8,128)(2,1)S(1)}, u32[]{:S(2)}, u32[]{:S(2)}) %collective-permute-start.1) | collective-permute-done | bytes 131104 | tf_op jit(solution)/shard_map/ppermute | solution.py:21
  82.3 1.4 pad_maximum_fusion.3
  83.7 1.4 pad_maximum_fusion.6
  85.1 1.4 pad_maximum_fusion.22
  86.5 1.5 pad_maximum_fusion.25
  88.0 1.6 fusion.90
  89.8 1.4 copy.12
  91.2 1.6 fusion.79
  99.7 4.6 %collective-permute-start.2 = (bf16[2,2,1,8,16,128]{5,4,3,2,1,0:T(8,128)(2,1)}, bf16[2,2,1,8,16,128]{5,4,3,2,1,0:T(8,128)(2,1)}, u32[]{:S(2)}, u32[]{:S(2)}) collective-permute-start(bf16[2,2,1,8,16,128]{5,4,3,2,1,0:T(8,128)(2,1)} %get-tuple-element.13), channel_id=1, source_target_pairs={{0,4},{4,8},{8,12},{12,16},{16,20},{20,24},{24,28},{28,32},{32,36}... | collective-permute-start | bytes 393224 | tf_op jit(solution)/shard_map/ppermute | solution.py:20
  104.6 1.4 copy.13
  115.7 3.8 %collective-permute-start.4 = (bf16[2,1,8,16,128]{4,3,2,1,0:T(8,128)(2,1)S(1)}, bf16[2,1,8,16,128]{4,3,2,1,0:T(8,128)(2,1)S(1)}, u32[]{:S(2)}, u32[]{:S(2)}) collective-permute-start(bf16[2,1,8,16,128]{4,3,2,1,0:T(8,128)(2,1)S(1)} %slice.703), channel_id=1, source_target_pairs={{0,4},{4,8},{8,12},{12,16},{16,20},{20,24},{24,28},{28,32},{32,36}... | collective-permute-start | bytes 196616 | tf_op jit(solution)/shard_map/ppermute | solution.py:29
  128.1 2.9 copy-done.2
  145.6 2.4 fusion.91
  148.0 5.2 %copy.15 = f32[27,256,128]{2,1,0:T(8,128)} copy(f32[27,256,128]{1,2,0:T(8,128)} %bitcast.179) | data formatting | bytes 7077888 | tf_op jit(solution)/shard_map/transpose | solution.py:134
  153.2 4.1 %constant_dynamic-update-slice_fusion.27 = f32[13824,128]{1,0:T(8,128)} fusion(f32[13824,128]{1,0:T(8,128)} %copy-done.2, f32[6912,128]{1,0:T(8,128)} %bitcast.178), kind=kLoop, calls=%fused_computation.285 | loop fusion | bytes 7077888 | tf_op jit(solution)/shard_map/concatenate | solution.py:177
  157.3 1.6 slice.704
  159.0 1.4 reshape.180
  160.4 2.6 copy.14
  164.1 162.9 %all-reduce.7.cloned.1.call-done = f32[13824,128]{1,0:T(8,128)} async-done(((f32[13824,128]{1,0:T(8,128)}), f32[13824,128]{1,0:T(8,128)}) %all-reduce.7.cloned.1.call-update) | async-done | bytes 7077904 | tf_op jit(solution)/shard_map/psum | solution.py:178
  327.0 1.5 divide_subtract_fusion
  (197 shorter events, 55.6 us)
Async XLA Ops:
  7.2 138.4 %copy-start = (bf16[1,2,2,4,8,256]{5,4,3,2,1,0:T(8,128)(2,1)S(1)}, bf16[1,2,2,4,8,256]{5,4,3,2,1,0:T(8,128)(2,1)}, u32[]{:S(2)}) copy-start(bf16[1,2,2,4,8,256]{5,4,3,2,1,0:T(8,128)(2,1)} %param.7) | copy-start | bytes 196612
  10.3 12.0 %copy-start.20 = (bf16[1,2,4,8,16,128]{5,4,3,2,1,0:T(8,128)(2,1)S(1)}, bf16[1,2,4,8,16,128]{5,4,3,2,1,0:T(8,128)(2,1)}, u32[]{:S(2)}) copy-start(bf16[1,2,4,8,16,128]{5,4,3,2,1,0:T(8,128)(2,1)} %param.9) | copy-start | bytes 786436
  10.3 12.0 %copy-start.1 = (bf16[1,2,4,8,16,128]{5,4,3,2,1,0:T(8,128)(2,1)S(1)}, bf16[1,2,4,8,16,128]{5,4,3,2,1,0:T(8,128)(2,1)}, u32[]{:S(2)}) copy-start(bf16[1,2,4,8,16,128]{5,4,3,2,1,0:T(8,128)(2,1)} %param.10) | copy-start | bytes 786436
  10.3 17.4 %copy-start.23 = (bf16[1,2,4,8,16,128]{5,4,3,2,1,0:T(8,128)(2,1)S(1)}, bf16[1,2,4,8,16,128]{5,4,3,2,1,0:T(8,128)(2,1)}, u32[]{:S(2)}) copy-start(bf16[1,2,4,8,16,128]{5,4,3,2,1,0:T(8,128)(2,1)} %param.8) | copy-start | bytes 786436
  10.3 77.7 %all-to-all-start = ((bf16[128,108,128]{2,1,0:T(8,128)(2,1)}), bf16[128,108,128]{2,1,0:T(8,128)(2,1)}, u32[]{:S(2)}, u32[]{:S(2)}) async-start(bf16[128,108,128]{2,1,0:T(8,128)(2,1)} %stack.7), calls=%async_computation | async-start | bytes 7340032 | tf_op jit(solution)/shard_map/all_to_all | solution.py:144
  22.2 304.8 %all-reduce.7.cloned.1.call-start = ((), (), s32[]{:S(2)}) async-start(), calls=%async_computation.1 | async-start | bytes 14155776 | tf_op jit(solution)/shard_map/psum | solution.py:178
  22.3 46.3 %collective-permute-start.1 = (bf16[2,2,1,8,16,128]{5,4,3,2,1,0:T(8,128)(2,1)S(1)}, bf16[2,2,1,8,16,128]{5,4,3,2,1,0:T(8,128)(2,1)S(1)}, u32[]{:S(2)}, u32[]{:S(2)}) collective-permute-start(bf16[2,2,1,8,16,128]{5,4,3,2,1,0:T(8,128)(2,1)S(1)} %get-tuple-element.16), channel_id=1, source_target_pairs={{4,0},{8,4},{12,8},{16,12},{20,16},{24,20},{28,24},{32,28},{36,32}... | collective-permute-start | bytes 393224 | tf_op jit(solution)/shard_map/ppermute | solution.py:21
  23.6 45.0 %collective-permute-start = (bf16[2,2,1,8,16,128]{5,4,3,2,1,0:T(8,128)(2,1)S(1)}, bf16[2,2,1,8,16,128]{5,4,3,2,1,0:T(8,128)(2,1)S(1)}, u32[]{:S(2)}, u32[]{:S(2)}) collective-permute-start(bf16[2,2,1,8,16,128]{5,4,3,2,1,0:T(8,128)(2,1)S(1)} %get-tuple-element.15), channel_id=1, source_target_pairs={{0,4},{4,8},{8,12},{12,16},{16,20},{20,24},{24,28},{28,32},{32,36}... | collective-permute-start | bytes 393224 | tf_op jit(solution)/shard_map/ppermute | solution.py:20
  91.2 1.6 copy-start.15
  91.2 2.0 copy-start.18
  98.4 7.7 %collective-permute-start.3 = (bf16[2,2,1,8,16,128]{5,4,3,2,1,0:T(8,128)(2,1)}, bf16[2,2,1,8,16,128]{5,4,3,2,1,0:T(8,128)(2,1)}, u32[]{:S(2)}, u32[]{:S(2)}) collective-permute-start(bf16[2,2,1,8,16,128]{5,4,3,2,1,0:T(8,128)(2,1)} %get-tuple-element.14), channel_id=1, source_target_pairs={{4,0},{8,4},{12,8},{16,12},{20,16},{24,20},{28,24},{32,28},{36,32}... | collective-permute-start | bytes 393224 | tf_op jit(solution)/shard_map/ppermute | solution.py:21
  99.7 6.4 %collective-permute-start.2 = (bf16[2,2,1,8,16,128]{5,4,3,2,1,0:T(8,128)(2,1)}, bf16[2,2,1,8,16,128]{5,4,3,2,1,0:T(8,128)(2,1)}, u32[]{:S(2)}, u32[]{:S(2)}) collective-permute-start(bf16[2,2,1,8,16,128]{5,4,3,2,1,0:T(8,128)(2,1)} %get-tuple-element.13), channel_id=1, source_target_pairs={{0,4},{4,8},{8,12},{12,16},{16,20},{20,24},{24,28},{28,32},{32,36}... | collective-permute-start | bytes 393224 | tf_op jit(solution)/shard_map/ppermute | solution.py:20
  104.6 1.5 copy-start.22
  115.7 15.4 %collective-permute-start.4 = (bf16[2,1,8,16,128]{4,3,2,1,0:T(8,128)(2,1)S(1)}, bf16[2,1,8,16,128]{4,3,2,1,0:T(8,128)(2,1)S(1)}, u32[]{:S(2)}, u32[]{:S(2)}) collective-permute-start(bf16[2,1,8,16,128]{4,3,2,1,0:T(8,128)(2,1)S(1)} %slice.703), channel_id=1, source_target_pairs={{0,4},{4,8},{8,12},{12,16},{16,20},{20,24},{24,28},{28,32},{32,36}... | collective-permute-start | bytes 196616 | tf_op jit(solution)/shard_map/ppermute | solution.py:29
  123.0 1.6 copy-start.7
  123.4 1.6 copy-start.11
  124.6 1.3 copy-start.5
  125.0 1.3 copy-start.12
  125.4 1.3 copy-start.10
  125.9 1.3 copy-start.3
  128.1 3.0 copy-start.2
  163.0 164.0 %copy-start.25 = (f32[108,128]{1,0:T(8,128)S(1)}, f32[108,128]{1,0:T(8,128)}, u32[]{:S(2)}) copy-start(f32[108,128]{1,0:T(8,128)} %param.11) | copy-start | bytes 165892
  163.0 164.0 %copy-start.26 = (f32[108,128]{1,0:T(8,128)S(1)}, f32[108,128]{1,0:T(8,128)}, u32[]{:S(2)}) copy-start(f32[108,128]{1,0:T(8,128)} %param.12) | copy-start | bytes 165892
  163.0 164.0 %copy-start.27 = (f32[108,128]{1,0:T(8,128)S(1)}, f32[108,128]{1,0:T(8,128)}, u32[]{:S(2)}) copy-start(f32[108,128]{1,0:T(8,128)} %param.13) | copy-start | bytes 165892
  (11 other events, 12.8 us)
Sparse Core Ops, SparseCore 0:
  157.5 169.5 all-reduce.6
